TPU v7x, 256 devices: a whole 4x4x8 slice. The times are simulated.
256 devices in a mesh: tm: 16 (over x_lo, z), expert: 16 (over y, x_hi, core).
Axes of the slice: x: 4 (x_hi: 2, x_lo: 2; x = x_hi * 2 + x_lo), y: 4, z: 8, core: 2. Of those that a mesh axis runs over, the one named last changes fastest.
Arguments:
- frames: float32 [32768, 1536], P(('tm', 'expert')), may hold values from -6 to 6
- lengths: int32 [2], replicated, may hold values from 1 to 24576, 32768 in all
- expert_ids: int32 [32768, 2], P(('tm', 'expert')), may hold values from 0 to 15, all different within a row; in each aligned block of 128 rows (0 to 127, 128 to 255, ...) at most 32 rows name the same one
- w_conv: float32 [31, 1536], replicated, may hold values from -1 to 1
- g_norm: float32 [1536], replicated, may hold values from 0.1 to 1.9
- w_router: float32 [1536, 16], replicated, may hold values from -0.15625 to 0.15625
- w_up: bfloat16 [16, 1536, 1536], P('expert'), may hold values from -0.15625 to 0.15625
- w_down: bfloat16 [16, 1536, 1536], P('expert'), may hold values from -0.15625 to 0.15625
- cotangent: float32 [32768, 1536], P(('tm', 'expert')), may hold values from -6 to 6
Outputs:
- block_out: float32 [32768, 1536], P(('tm', 'expert'))
- frames_grad: float32 [32768, 1536], P(('tm', 'expert'))
- conv_grad: float32 [31, 1536], replicated
- gain_grad: float32 [1536], replicated
- router_grad: float32 [1536, 16], replicated
Inputs may be any that keep to these rules, and one draw needn't show every extreme that they name: `expert_ids`: within the frames of one device (aligned blocks of 128 frames) no expert is named more than 32 times, a bound that some block reaches. The two experts of a frame differ. The lengths sum to 32768; the longest is at most 24576.
All inputs are finite; a program needn't handle non-finite values.
Results may differ from a plain program's by a relative error of at most 0.02.
Values may be sent and summed in bfloat16 or wider, within the bound.
A program may use at most 128 MiB of HBM per device.

v0:
```python
import jax
import jax.numpy as jnp
from jax import lax
from jax.sharding import PartitionSpec as P

EPS = 1e-06


def with_halo(block, sides, width):
    for axis, dim in sides:
        count = lax.axis_size(axis)
        forward = [(i, i + 1) for i in range(count - 1)]
        backward = [(target, source) for source, target in forward]
        low = lax.ppermute(
            lax.slice_in_dim(block, block.shape[dim] - width, None, axis=dim), axis, forward
        )
        high = lax.ppermute(lax.slice_in_dim(block, 0, width, axis=dim), axis, backward)
        block = jnp.concatenate([low, block, high], axis=dim)
    return block


def recording_of(position, lengths):
    bounds = jnp.cumsum(lengths)[:-1]
    return jnp.sum((position[:, None] >= bounds[None, :]).astype(jnp.int32), axis=1)


def conv_terms(widened, labels, w_conv, frame_count):
    kernel_len = w_conv.shape[0]
    half_width = (kernel_len - 1) // 2
    middle = labels[half_width : half_width + frame_count]
    summed = jnp.zeros((frame_count, widened.shape[1]), jnp.float32)
    for offset in range(kernel_len):
        matching = (labels[offset : offset + frame_count] == middle).astype(jnp.float32)
        summed = (
            summed
            + w_conv[offset][None, :] * widened[offset : offset + frame_count] * matching[:, None]
        )
    return summed


def norm_rows(mixed, g_norm):
    inv_scale = lax.rsqrt(jnp.mean(mixed * mixed, axis=-1, keepdims=True) + EPS)
    return (mixed * inv_scale * g_norm[None, :]).astype(jnp.bfloat16)


def mix_rows(mixed, normed, picked, w_router, expert_ids):
    logits = jnp.dot(normed, w_router, precision=lax.Precision.HIGHEST)
    expert_count = w_router.shape[1]
    chosen = (
        expert_ids[:, :, None] == jnp.arange(expert_count, dtype=jnp.int32)[None, None, :]
    ).astype(jnp.float32)
    top_logits = jnp.einsum("fke,fe->fk", chosen, logits, precision=lax.Precision.HIGHEST)
    gate_weights = jax.nn.softmax(top_logits, axis=-1)
    return mixed + jnp.sum(gate_weights[:, :, None] * picked.astype(jnp.float32), axis=1)


def slot_positions(route_rows, expert_count, capacity):
    flat_ids = route_rows.reshape(-1)
    matches = (flat_ids[:, None] == jnp.arange(expert_count, dtype=jnp.int32)[None, :]).astype(
        jnp.int32
    )
    before = jnp.cumsum(matches, axis=0) - matches
    slot_index = jnp.sum(before * matches, axis=1)
    return flat_ids * capacity + slot_index


def expert_rows(rows_in, w_up, w_down):
    hidden = jax.nn.silu(
        jnp.einsum("sjcd,jdf->sjcf", rows_in, w_up, preferred_element_type=jnp.float32)
    ).astype(jnp.bfloat16)
    return jnp.einsum("sjcf,jfd->sjcd", hidden, w_down, preferred_element_type=jnp.float32).astype(
        jnp.bfloat16
    )


def widen_rows(field, half_width):
    return with_halo(field.astype(jnp.bfloat16), ((("tm", "expert"), 0),), half_width).astype(
        field.dtype
    )


def trade_rows(buffer):
    return lax.all_to_all(buffer, "expert", split_axis=0, concat_axis=0, tiled=True)


def on_device(frames, lengths, expert_ids, w_conv, g_norm, w_router, w_up, w_down, cotangent):
    frame_count, feature_count = frames.shape
    expert_count = w_router.shape[1]
    local_count = w_up.shape[0]
    peer_count = lax.axis_size("expert")
    capacity = 2 * (2 * frame_count // expert_count)
    kernel_len = w_conv.shape[0]
    half_width = (kernel_len - 1) // 2
    device = lax.axis_index("tm") * peer_count + lax.axis_index("expert")
    first_row = device * frame_count
    labels = recording_of(
        first_row - half_width + jnp.arange(frame_count + 2 * half_width, dtype=jnp.int32), lengths
    )
    middle = labels[half_width : half_width + frame_count]
    widened = widen_rows(frames, half_width)
    pre_act = conv_terms(widened, labels, w_conv, frame_count)
    mixed = frames + jax.nn.silu(pre_act)

    def norm_float(mixed_in, gain_in):
        return norm_rows(mixed_in, gain_in).astype(jnp.float32)

    normed, norm_back = jax.vjp(norm_float, mixed, g_norm)
    positions = slot_positions(expert_ids, expert_count, capacity)
    assigned = jnp.broadcast_to(normed[:, None, :], (frame_count, 2, feature_count))
    assigned = assigned.reshape(2 * frame_count, feature_count).astype(jnp.bfloat16)
    outgoing = (
        jnp.zeros((expert_count * capacity, feature_count), jnp.bfloat16)
        .at[positions]
        .set(assigned)
    )
    received = trade_rows(outgoing.reshape(peer_count, local_count * capacity, feature_count))
    received = received.reshape(peer_count, local_count, capacity, feature_count)

    def apply_experts(rows_in):
        return expert_rows(rows_in, w_up, w_down)

    results, expert_back = jax.vjp(apply_experts, received)
    returned = trade_rows(results.reshape(peer_count, local_count * capacity, feature_count))
    returned = returned.reshape(expert_count * capacity, feature_count)
    picked = returned[positions].reshape(frame_count, 2, feature_count)

    def mix_local(mixed_in, normed_in, picked_in, router_in):
        return mix_rows(mixed_in, normed_in, picked_in, router_in, expert_ids)

    block_out, mix_back = jax.vjp(mix_local, mixed, normed, picked, w_router)
    d_mixed, d_normed, d_picked, d_router = mix_back(cotangent)
    sent_back = jnp.zeros((expert_count * capacity, feature_count), jnp.bfloat16)
    sent_back = sent_back.at[positions].set(d_picked.reshape(2 * frame_count, feature_count))
    arriving = trade_rows(sent_back.reshape(peer_count, local_count * capacity, feature_count))
    arriving = arriving.reshape(peer_count, local_count, capacity, feature_count)
    (d_rows,) = expert_back(arriving)
    came_back = trade_rows(d_rows.reshape(peer_count, local_count * capacity, feature_count))
    came_back = came_back.reshape(expert_count * capacity, feature_count)
    row_grads = came_back[positions].astype(jnp.float32).reshape(frame_count, 2, feature_count)
    d_normed = d_normed + jnp.sum(row_grads, axis=1)
    d_mixed_norm, d_gain = norm_back(d_normed)
    d_mixed = d_mixed + d_mixed_norm
    sigmoid_pre = jax.nn.sigmoid(pre_act)
    d_pre = d_mixed * sigmoid_pre * (1.0 + pre_act * (1.0 - sigmoid_pre))
    d_wide = widen_rows(d_pre, half_width)
    d_frames = d_mixed
    kernel_rows = []
    for offset in range(kernel_len):
        matching = (labels[offset : offset + frame_count] == middle).astype(jnp.float32)[:, None]
        d_frames = (
            d_frames
            + w_conv[kernel_len - 1 - offset][None, :]
            * d_wide[offset : offset + frame_count]
            * matching
        )
        kernel_rows.append(
            jnp.sum(d_pre * widened[offset : offset + frame_count] * matching, axis=0)
        )
    d_kernel = jnp.stack(kernel_rows, axis=0)
    d_kernel, d_gain, d_router = lax.psum((d_kernel, d_gain, d_router), ("tm", "expert"))
    return (block_out, d_frames, d_kernel, d_gain, d_router)


def solution(mesh):
    placed = (
        P(("tm", "expert"), None),
        P(),
        P(("tm", "expert"), None),
        P(),
        P(),
        P(),
        P("expert", None, None),
        P("expert", None, None),
        P(("tm", "expert"), None),
    )
    return jax.shard_map(
        on_device,
        mesh=mesh,
        in_specs=placed,
        out_specs=(P(("tm", "expert"), None), P(("tm", "expert"), None), P(), P(), P()),
        check_vma=False,
    )
```

profile of v0, /device:TPU:1, one launch (start us, length us, event | category | flops | bytes accessed | tf_op | source)
XLA Modules:
  0.0 454.0 jit_solution(14232007829993305681)
XLA Ops:
  7.2 1.2 convert_element_type.185
  8.5 6.2 %collective-permute-start = (bf16[15,1536]{1,0:T(8,128)(2,1)S(1)}, bf16[15,1536]{1,0:T(8,128)(2,1)S(1)}, u32[]{:S(2)}, u32[]{:S(2)}) collective-permute-start(bf16[15,1536]{1,0:T(8,128)(2,1)S(1)} %get-tuple-element.82), channel_id=1, source_target_pairs={{0,1},{1,2},{2,3},{3,4},{4,5},{5,6},{6,7},{7,8},{8,9},{9,10},{10,1... | collective-permute-start | bytes 138248 | tf_op jit(solution)/shard_map/ppermute | solution.py:14
  14.6 1.9 collective-permute-start.1
  16.6 0.8 reduce-window.10
  17.7 0.7 fusion.121
  18.4 0.7 fusion.120
  19.1 0.7 broadcast_multiply_fusion
  19.8 0.8 copy.15
  21.1 0.6 reduce-window.11
  22.5 0.6 compare_select_fusion
  23.5 8.0 %multiply_reduce_fusion.35 = (f32[128]{0:T(128)}, f32[128,1536]{1,0:T(8,128)S(1)}, f32[128,1536]{1,0:T(8,128)}) fusion(f32[128,1536]{1,0:T(8,128)S(1)} %copy-done.6, f32[128]{0:T(128)S(1)} %get-tuple-element.113, f32[158,1536]{1,0:T(8,128)S(1)} %maximum_convert_fusion, f32[1536]{0:T(1024)S(1)} %get-tuple-element.69, f32[128]{0:T(128)} %get-tuple-element.85, ...), kind=kLoop, calls=%fused_computation.168 | loop fusion | flops 19267456 | bytes 26945024 | tf_op jit(solution)/shard_map/jvp()/reduce_sum | solution.py:42
  31.9 0.6 fusion.150
  32.7 0.4 copy-done.96
  33.0 0.7 copy-done.3
  33.8 0.4 broadcast_in_dim.12
  34.5 3.3 scatter_custom_fusion
  37.8 8.2 %all-to-all-start = ((bf16[16,32,1536]{2,1,0:T(8,128)(2,1)}), bf16[16,32,1536]{2,1,0:T(8,128)(2,1)}, u32[]{:S(2)}, u32[]{:S(2)}) async-start(bf16[16,32,1536]{2,1,0:T(8,128)(2,1)} %bitcast.170), calls=%async_computation | async-start | bytes 3145728 | tf_op jit(solution)/shard_map/all_to_all | solution.py:83
  46.0 1.7 broadcast_in_dim.13
  47.7 2.4 broadcast_in_dim.16
  50.0 1.4 fusion.156
  51.5 1.5 fusion.111
  53.0 0.7 reduce_max.9
  53.7 0.8 fusion.115
  54.5 0.5 copy-done.98
  55.1 1.4 fusion.114
  56.5 1.5 mul.1750
  58.0 3.4 scatter_custom_fusion.1
  61.4 7.4 %all-to-all-done = bf16[16,32,1536]{2,1,0:T(8,128)(2,1)} async-done(((bf16[16,32,1536]{2,1,0:T(8,128)(2,1)}), bf16[16,32,1536]{2,1,0:T(8,128)(2,1)}, u32[]{:S(2)}, u32[]{:S(2)}) %all-to-all-start) | async-done | bytes 1572896 | tf_op jit(solution)/shard_map/all_to_all | solution.py:83
  68.8 4.4 all-to-all-start.2
  73.2 4.9 %fusion.8 = f32[16,1,32,1536]{3,2,0,1:T(8,128)S(1)} fusion(bf16[16,32,1536]{2,1,0:T(8,128)(2,1)} %all-to-all-done, bf16[1,1536,1536]{2,1,0:T(8,128)(2,1)} %param.15), kind=kOutput, calls=%fused_computation.15 | convolution fusion | flops 2415919104 | bytes 9437184 | tf_op jit(solution)/shard_map/jvp(sjcd,jdf->sjcf)/dot_general | solution.py:69
  78.2 1.7 copy-done.101
  79.8 6.2 %fusion.16 = bf16[16,32,1536]{2,1,0:T(8,128)(2,1)} fusion(bf16[1,1536,1536]{2,1,0:T(8,128)(2,1)} %param.16, f32[16,1,32,1536]{3,2,0,1:T(8,128)S(1)} %fusion.8), kind=kOutput, calls=%fused_computation.21 | convolution fusion | flops 2420637696 | bytes 9437184 | tf_op jit(solution)/shard_map/jvp(sjcf,jfd->sjcd)/dot_general | solution.py:71
  86.0 10.2 %all-to-all-done.2 = bf16[16,32,1536]{2,1,0:T(8,128)(2,1)S(1)} async-done(((bf16[16,32,1536]{2,1,0:T(8,128)(2,1)}), bf16[16,32,1536]{2,1,0:T(8,128)(2,1)S(1)}, u32[]{:S(2)}, u32[]{:S(2)}) %all-to-all-start.2) | async-done | bytes 1572896 | tf_op jit(solution)/shard_map/all_to_all | solution.py:83
  96.2 1.1 copy-done.8
  97.3 4.4 all-to-all-start.1
  101.7 11.5 %fusion.22 = bf16[16,32,1536]{2,1,0:T(8,128)(2,1)} fusion(bf16[1,1536,1536]{2,1,0:T(8,128)(2,1)} %param.15, f32[16,1,32,1536]{3,2,0,1:T(8,128)} %copy-done.101, bf16[1,1536,1536]{2,1,0:T(8,128)(2,1)} %param.16, bf16[16,32,1536]{2,1,0:T(8,128)(2,1)} %copy-done.8), kind=kOutput, calls=%fused_computation.23 | convolution fusion | flops 4841275392 | bytes 15728640 | tf_op jit(solution)/shard_map/transpose(jvp(sjcd,jdf->sjcf))/dot_general | solution.py:69
  113.2 11.4 %all-to-all-done.1 = bf16[16,32,1536]{2,1,0:T(8,128)(2,1)S(1)} async-done(((bf16[16,32,1536]{2,1,0:T(8,128)(2,1)}), bf16[16,32,1536]{2,1,0:T(8,128)(2,1)S(1)}, u32[]{:S(2)}, u32[]{:S(2)}) %all-to-all-start.1) | async-done | bytes 1572896 | tf_op jit(solution)/shard_map/all_to_all | solution.py:83
  124.7 5.0 %all-to-all-start.3 = ((bf16[16,32,1536]{2,1,0:T(8,128)(2,1)}), bf16[16,32,1536]{2,1,0:T(8,128)(2,1)}, u32[]{:S(2)}, u32[]{:S(2)}) async-start(bf16[16,32,1536]{2,1,0:T(8,128)(2,1)} %fusion.22), calls=%async_computation.3 | async-start | bytes 3145728 | tf_op jit(solution)/shard_map/all_to_all | solution.py:83
  129.7 11.0 %all-reduce.3.cloned.1.call-start = ((), (), s32[]{:S(2)}) async-start(), calls=%async_computation.4 | async-start | bytes 589824 | tf_op jit(solution)/shard_map/psum | solution.py:160
  140.7 1.3 pad_clamp_fusion
  142.0 1.1 multiply_divide_fusion
  143.1 2.3 gather_fusion
  145.4 7.3 %all-to-all-done.3 = bf16[16,32,1536]{2,1,0:T(8,128)(2,1)} async-done(((bf16[16,32,1536]{2,1,0:T(8,128)(2,1)}), bf16[16,32,1536]{2,1,0:T(8,128)(2,1)}, u32[]{:S(2)}, u32[]{:S(2)}) %all-to-all-start.3) | async-done | bytes 1572896 | tf_op jit(solution)/shard_map/all_to_all | solution.py:83
  152.8 3.7 gather_fusion.1
  156.5 2.1 reshape.264
  158.6 2.1 reshape.262
  160.8 4.8 %multiply_reduce_fusion = (f32[128,2]{1,0:T(8,128)S(1)}, f32[128,1536]{1,0:T(8,128)}) fusion(f32[128,2,1536]{2,1,0:T(2,128)} %reshape.262, f32[128,1536]{1,0:T(8,128)S(1)} %copy-done.2, f32[128,2]{1,0:T(8,128)} %fusion.114), kind=kLoop, calls=%fused_computation.31 | loop fusion | flops 1376000 | bytes 3147776 | tf_op jit(solution)/shard_map/transpose(jvp())/reduce_sum | solution.py:54
  165.9 0.6 fusion.110
  166.5 3.3 reduce_sum.389
  169.8 3.6 multiply_reduce_fusion.2
  173.5 0.6 multiply_multiply_fusion
  174.2 2.8 multiply_reduce_fusion.3
  177.1 1.2 multiply_reduce_fusion.30
  178.4 1.5 multiply_reduce_fusion.21
  179.9 2.2 multiply_reduce_fusion.12
  182.1 3.2 collective-permute-start.2
  185.6 2.1 collective-permute-start.3
  187.7 1.0 fusion.157
  189.1 2.8 stack.127
  191.8 83.7 %psum.22 = f32[1536]{0:T(1024)} all-reduce(f32[1536]{0:T(1024)S(1)} %copy-done.64), channel_id=1, replica_groups=mesh['tm'=16,'expert'=16] {'tm','expert'}, use_global_device_ids=true, to_apply=%region_47.48 | all-reduce | flops 1536 | bytes 12288 | tf_op jit(solution)/shard_map/psum | solution.py:160
  276.0 5.7 %fusion.46 = f32[128,1536]{1,0:T(8,128)} fusion(f32[158,1536]{1,0:T(8,128)S(1)} %maximum_convert_fusion.1, f32[128,1536]{1,0:T(8,128)S(1)} %get-tuple-element.74, f32[128]{0:T(128)S(1)} %copy-done.73, f32[1536]{0:T(1024)S(1)} %copy-done.59, f32[128]{0:T(128)} %get-tuple-element.85, f32[1536]{0:T(1024)S(1)} %copy-done.61, f32[128]{0:T(128)} %get-tuple-element.86, ...), kind=kLoop, calls=%fused_computation.39 | loop fusion | flops 18087936 | bytes 26158080 | tf_op jit(solution)/shard_map/add | solution.py:151
  281.7 162.1 %all-reduce.3.cloned.1.call-done = (f32[31,1536]{1,0:T(8,128)}, f32[1536,16]{0,1:T(8,128)}) async-done(((f32[31,1536]{1,0:T(8,128)}, f32[1536,16]{0,1:T(8,128)}), (f32[31,1536]{1,0:T(8,128)}, f32[1536,16]{0,1:T(8,128)})) %all-reduce.3.cloned.1.call-update) | async-done | bytes 288784 | tf_op jit(solution)/shard_map/psum | solution.py:160
  443.8 1.6 copy.28
  445.4 1.5 copy.29
  (258 shorter events, 3.2 us)
Async XLA Ops:
  7.2 42.9 %copy-start = (f32[1536,16]{0,1:T(8,128)S(1)}, f32[1536,16]{0,1:T(8,128)}, u32[]{:S(2)}) copy-start(f32[1536,16]{0,1:T(8,128)} %param.14) | copy-start | bytes 294916
  7.2 14.8 %copy-start.11 = (f32[31,1536]{1,0:T(8,128)S(1)}, f32[31,1536]{1,0:T(8,128)}, u32[]{:S(2)}) copy-start(f32[31,1536]{1,0:T(8,128)} %param.12) | copy-start | bytes 571396
  8.4 15.1 %copy-start.6 = (f32[128,1536]{1,0:T(8,128)S(1)}, f32[128,1536]{1,0:T(8,128)}, u32[]{:S(2)}) copy-start(f32[128,1536]{1,0:T(8,128)} %param.9) | copy-start | bytes 2359300
  8.5 14.9 %collective-permute-start = (bf16[15,1536]{1,0:T(8,128)(2,1)S(1)}, bf16[15,1536]{1,0:T(8,128)(2,1)S(1)}, u32[]{:S(2)}, u32[]{:S(2)}) collective-permute-start(bf16[15,1536]{1,0:T(8,128)(2,1)S(1)} %get-tuple-element.82), channel_id=1, source_target_pairs={{0,1},{1,2},{2,3},{3,4},{4,5},{5,6},{6,7},{7,8},{8,9},{9,10},{10,1... | collective-permute-start | bytes 138248 | tf_op jit(solution)/shard_map/ppermute | solution.py:14
  14.6 8.7 %collective-permute-start.1 = (bf16[15,1536]{1,0:T(8,128)(2,1)S(1)}, bf16[15,1536]{1,0:T(8,128)(2,1)S(1)}, u32[]{:S(2)}, u32[]{:S(2)}) collective-permute-start(bf16[15,1536]{1,0:T(8,128)(2,1)S(1)} %get-tuple-element.83), channel_id=1, source_target_pairs={{1,0},{2,1},{3,2},{4,3},{5,4},{6,5},{7,6},{8,7},{9,8},{10,9},{11,1... | collective-permute-start | bytes 138248 | tf_op jit(solution)/shard_map/ppermute | solution.py:17
  17.5 14.0 %copy-start.66 = (f32[128]{0:T(128)}, f32[128]{0:T(128)S(1)}, u32[]{:S(2)}) copy-start(f32[128]{0:T(128)S(1)} %get-tuple-element.111) | copy-start | bytes 1540
  17.5 14.0 %copy-start.69 = (f32[128]{0:T(128)}, f32[128]{0:T(128)S(1)}, u32[]{:S(2)}) copy-start(f32[128]{0:T(128)S(1)} %get-tuple-element.112) | copy-start | bytes 1540
  17.5 14.0 %copy-start.71 = (f32[128]{0:T(128)}, f32[128]{0:T(128)S(1)}, u32[]{:S(2)}) copy-start(f32[128]{0:T(128)S(1)} %get-tuple-element.113) | copy-start | bytes 1540
  17.6 13.9 %copy-start.74 = (f32[128]{0:T(128)}, f32[128]{0:T(128)S(1)}, u32[]{:S(2)}) copy-start(f32[128]{0:T(128)S(1)} %get-tuple-element.102) | copy-start | bytes 1540
  17.6 13.9 %copy-start.77 = (f32[128]{0:T(128)}, f32[128]{0:T(128)S(1)}, u32[]{:S(2)}) copy-start(f32[128]{0:T(128)S(1)} %get-tuple-element.103) | copy-start | bytes 1540
  17.6 13.9 %copy-start.79 = (f32[128]{0:T(128)}, f32[128]{0:T(128)S(1)}, u32[]{:S(2)}) copy-start(f32[128]{0:T(128)S(1)} %get-tuple-element.104) | copy-start | bytes 1540
  17.6 13.9 %copy-start.81 = (f32[128]{0:T(128)}, f32[128]{0:T(128)S(1)}, u32[]{:S(2)}) copy-start(f32[128]{0:T(128)S(1)} %get-tuple-element.105) | copy-start | bytes 1540
  17.7 13.9 %copy-start.83 = (f32[128]{0:T(128)}, f32[128]{0:T(128)S(1)}, u32[]{:S(2)}) copy-start(f32[128]{0:T(128)S(1)} %get-tuple-element.106) | copy-start | bytes 1540
  17.7 13.9 %copy-start.85 = (f32[128]{0:T(128)}, f32[128]{0:T(128)S(1)}, u32[]{:S(2)}) copy-start(f32[128]{0:T(128)S(1)} %get-tuple-element.107) | copy-start | bytes 1540
  17.7 13.9 %copy-start.87 = (f32[128]{0:T(128)}, f32[128]{0:T(128)S(1)}, u32[]{:S(2)}) copy-start(f32[128]{0:T(128)S(1)} %get-tuple-element.108) | copy-start | bytes 1540
  17.7 13.9 %copy-start.89 = (f32[128]{0:T(128)}, f32[128]{0:T(128)S(1)}, u32[]{:S(2)}) copy-start(f32[128]{0:T(128)S(1)} %get-tuple-element.109) | copy-start | bytes 1540
  17.7 13.9 %copy-start.91 = (f32[128]{0:T(128)}, f32[128]{0:T(128)S(1)}, u32[]{:S(2)}) copy-start(f32[128]{0:T(128)S(1)} %get-tuple-element.110) | copy-start | bytes 1540
  18.4 13.2 %copy-start.93 = (f32[128]{0:T(128)}, f32[128]{0:T(128)S(1)}, u32[]{:S(2)}) copy-start(f32[128]{0:T(128)S(1)} %get-tuple-element.93) | copy-start | bytes 1540
  22.3 9.4 %copy-start.12 = (f32[1536]{0:T(1024)}, f32[1536]{0:T(1024)S(1)}, u32[]{:S(2)}) copy-start(f32[1536]{0:T(1024)S(1)} %get-tuple-element.46) | copy-start | bytes 18436
  22.3 9.4 %copy-start.14 = (f32[1536]{0:T(1024)}, f32[1536]{0:T(1024)S(1)}, u32[]{:S(2)}) copy-start(f32[1536]{0:T(1024)S(1)} %get-tuple-element.47) | copy-start | bytes 18436
  22.3 9.4 %copy-start.16 = (f32[1536]{0:T(1024)}, f32[1536]{0:T(1024)S(1)}, u32[]{:S(2)}) copy-start(f32[1536]{0:T(1024)S(1)} %get-tuple-element.48) | copy-start | bytes 18436
  22.3 9.4 %copy-start.18 = (f32[1536]{0:T(1024)}, f32[1536]{0:T(1024)S(1)}, u32[]{:S(2)}) copy-start(f32[1536]{0:T(1024)S(1)} %get-tuple-element.49) | copy-start | bytes 18436
  22.3 9.4 %copy-start.20 = (f32[1536]{0:T(1024)}, f32[1536]{0:T(1024)S(1)}, u32[]{:S(2)}) copy-start(f32[1536]{0:T(1024)S(1)} %get-tuple-element.50) | copy-start | bytes 18436
  22.3 9.4 %copy-start.22 = (f32[1536]{0:T(1024)}, f32[1536]{0:T(1024)S(1)}, u32[]{:S(2)}) copy-start(f32[1536]{0:T(1024)S(1)} %get-tuple-element.51) | copy-start | bytes 18436
  22.3 9.4 %copy-start.24 = (f32[1536]{0:T(1024)}, f32[1536]{0:T(1024)S(1)}, u32[]{:S(2)}) copy-start(f32[1536]{0:T(1024)S(1)} %get-tuple-element.52) | copy-start | bytes 18436
  22.3 9.4 %copy-start.26 = (f32[1536]{0:T(1024)}, f32[1536]{0:T(1024)S(1)}, u32[]{:S(2)}) copy-start(f32[1536]{0:T(1024)S(1)} %get-tuple-element.53) | copy-start | bytes 18436
  22.3 9.4 %copy-start.28 = (f32[1536]{0:T(1024)}, f32[1536]{0:T(1024)S(1)}, u32[]{:S(2)}) copy-start(f32[1536]{0:T(1024)S(1)} %get-tuple-element.54) | copy-start | bytes 18436
  37.8 31.0 %all-to-all-start = ((bf16[16,32,1536]{2,1,0:T(8,128)(2,1)}), bf16[16,32,1536]{2,1,0:T(8,128)(2,1)}, u32[]{:S(2)}, u32[]{:S(2)}) async-start(bf16[16,32,1536]{2,1,0:T(8,128)(2,1)} %bitcast.170), calls=%async_computation | async-start | bytes 3145728 | tf_op jit(solution)/shard_map/all_to_all | solution.py:83
  68.8 27.4 %all-to-all-start.2 = ((bf16[16,32,1536]{2,1,0:T(8,128)(2,1)}), bf16[16,32,1536]{2,1,0:T(8,128)(2,1)S(1)}, u32[]{:S(2)}, u32[]{:S(2)}) async-start(bf16[16,32,1536]{2,1,0:T(8,128)(2,1)} %bitcast.55), calls=%async_computation.2 | async-start | bytes 3145728 | tf_op jit(solution)/shard_map/all_to_all | solution.py:83
  97.3 27.4 %all-to-all-start.1 = ((bf16[16,32,1536]{2,1,0:T(8,128)(2,1)}), bf16[16,32,1536]{2,1,0:T(8,128)(2,1)S(1)}, u32[]{:S(2)}, u32[]{:S(2)}) async-start(bf16[16,32,1536]{2,1,0:T(8,128)(2,1)} %fusion.16), calls=%async_computation.1 | async-start | bytes 3145728 | tf_op jit(solution)/shard_map/all_to_all | solution.py:83
  124.7 28.1 %all-to-all-start.3 = ((bf16[16,32,1536]{2,1,0:T(8,128)(2,1)}), bf16[16,32,1536]{2,1,0:T(8,128)(2,1)}, u32[]{:S(2)}, u32[]{:S(2)}) async-start(bf16[16,32,1536]{2,1,0:T(8,128)(2,1)} %fusion.22), calls=%async_computation.3 | async-start | bytes 3145728 | tf_op jit(solution)/shard_map/all_to_all | solution.py:83
  129.7 314.1 %all-reduce.3.cloned.1.call-start = ((), (), s32[]{:S(2)}) async-start(), calls=%async_computation.4 | async-start | bytes 589824 | tf_op jit(solution)/shard_map/psum | solution.py:160
  182.1 9.8 %copy-start.64 = (f32[1536]{0:T(1024)S(1)}, f32[1536]{0:T(1024)}, u32[]{:S(2)}) copy-start(f32[1536]{0:T(1024)} %get-tuple-element.36) | copy-start | bytes 18436
  182.1 93.4 %collective-permute-start.2 = (bf16[15,1536]{1,0:T(8,128)(2,1)S(1)}, bf16[15,1536]{1,0:T(8,128)(2,1)S(1)}, u32[]{:S(2)}, u32[]{:S(2)}) collective-permute-start(bf16[15,1536]{1,0:T(8,128)(2,1)S(1)} %get-tuple-element.80), channel_id=1, source_target_pairs={{0,1},{1,2},{2,3},{3,4},{4,5},{5,6},{6,7},{7,8},{8,9},{9,10},{10,1... | collective-permute-start | bytes 138248 | tf_op jit(solution)/shard_map/ppermute | solution.py:14
  185.3 90.4 %copy-start.13 = (f32[1536]{0:T(1024)S(1)}, f32[1536]{0:T(1024)}, u32[]{:S(2)}) copy-start(f32[1536]{0:T(1024)} %copy-done.12) | copy-start | bytes 18436
  185.3 90.4 %copy-start.15 = (f32[1536]{0:T(1024)S(1)}, f32[1536]{0:T(1024)}, u32[]{:S(2)}) copy-start(f32[1536]{0:T(1024)} %copy-done.14) | copy-start | bytes 18436
  185.3 90.4 %copy-start.17 = (f32[1536]{0:T(1024)S(1)}, f32[1536]{0:T(1024)}, u32[]{:S(2)}) copy-start(f32[1536]{0:T(1024)} %copy-done.16) | copy-start | bytes 18436
  185.3 90.4 %copy-start.19 = (f32[1536]{0:T(1024)S(1)}, f32[1536]{0:T(1024)}, u32[]{:S(2)}) copy-start(f32[1536]{0:T(1024)} %copy-done.18) | copy-start | bytes 18436
  185.3 90.4 %copy-start.21 = (f32[1536]{0:T(1024)S(1)}, f32[1536]{0:T(1024)}, u32[]{:S(2)}) copy-start(f32[1536]{0:T(1024)} %copy-done.20) | copy-start | bytes 18436
  185.3 90.4 %copy-start.23 = (f32[1536]{0:T(1024)S(1)}, f32[1536]{0:T(1024)}, u32[]{:S(2)}) copy-start(f32[1536]{0:T(1024)} %copy-done.22) | copy-start | bytes 18436
  185.4 90.4 %copy-start.25 = (f32[1536]{0:T(1024)S(1)}, f32[1536]{0:T(1024)}, u32[]{:S(2)}) copy-start(f32[1536]{0:T(1024)} %copy-done.24) | copy-start | bytes 18436
  185.4 90.4 %copy-start.27 = (f32[1536]{0:T(1024)S(1)}, f32[1536]{0:T(1024)}, u32[]{:S(2)}) copy-start(f32[1536]{0:T(1024)} %copy-done.26) | copy-start | bytes 18436
  185.4 90.4 %copy-start.29 = (f32[1536]{0:T(1024)S(1)}, f32[1536]{0:T(1024)}, u32[]{:S(2)}) copy-start(f32[1536]{0:T(1024)} %copy-done.28) | copy-start | bytes 18436
  185.4 90.4 %copy-start.31 = (f32[1536]{0:T(1024)S(1)}, f32[1536]{0:T(1024)}, u32[]{:S(2)}) copy-start(f32[1536]{0:T(1024)} %copy-done.30) | copy-start | bytes 18436
  185.4 90.4 %copy-start.33 = (f32[1536]{0:T(1024)S(1)}, f32[1536]{0:T(1024)}, u32[]{:S(2)}) copy-start(f32[1536]{0:T(1024)} %copy-done.32) | copy-start | bytes 18436
  185.4 90.4 %copy-start.35 = (f32[1536]{0:T(1024)S(1)}, f32[1536]{0:T(1024)}, u32[]{:S(2)}) copy-start(f32[1536]{0:T(1024)} %copy-done.34) | copy-start | bytes 18436
  185.4 90.4 %copy-start.37 = (f32[1536]{0:T(1024)S(1)}, f32[1536]{0:T(1024)}, u32[]{:S(2)}) copy-start(f32[1536]{0:T(1024)} %copy-done.36) | copy-start | bytes 18436
  185.4 90.4 %copy-start.39 = (f32[1536]{0:T(1024)S(1)}, f32[1536]{0:T(1024)}, u32[]{:S(2)}) copy-start(f32[1536]{0:T(1024)} %copy-done.38) | copy-start | bytes 18436
  185.4 90.4 %copy-start.41 = (f32[1536]{0:T(1024)S(1)}, f32[1536]{0:T(1024)}, u32[]{:S(2)}) copy-start(f32[1536]{0:T(1024)} %copy-done.40) | copy-start | bytes 18436
  185.4 90.4 %copy-start.43 = (f32[1536]{0:T(1024)S(1)}, f32[1536]{0:T(1024)}, u32[]{:S(2)}) copy-start(f32[1536]{0:T(1024)} %copy-done.42) | copy-start | bytes 18436
  185.5 90.4 %copy-start.45 = (f32[1536]{0:T(1024)S(1)}, f32[1536]{0:T(1024)}, u32[]{:S(2)}) copy-start(f32[1536]{0:T(1024)} %copy-done.44) | copy-start | bytes 18436
  185.5 90.4 %copy-start.47 = (f32[1536]{0:T(1024)S(1)}, f32[1536]{0:T(1024)}, u32[]{:S(2)}) copy-start(f32[1536]{0:T(1024)} %copy-done.46) | copy-start | bytes 18436
  185.5 90.4 %copy-start.49 = (f32[1536]{0:T(1024)S(1)}, f32[1536]{0:T(1024)}, u32[]{:S(2)}) copy-start(f32[1536]{0:T(1024)} %copy-done.48) | copy-start | bytes 18436
  185.5 90.4 %copy-start.51 = (f32[1536]{0:T(1024)S(1)}, f32[1536]{0:T(1024)}, u32[]{:S(2)}) copy-start(f32[1536]{0:T(1024)} %copy-done.50) | copy-start | bytes 18436
  185.5 90.4 %copy-start.53 = (f32[1536]{0:T(1024)S(1)}, f32[1536]{0:T(1024)}, u32[]{:S(2)}) copy-start(f32[1536]{0:T(1024)} %copy-done.52) | copy-start | bytes 18436
  185.5 90.4 %copy-start.55 = (f32[1536]{0:T(1024)S(1)}, f32[1536]{0:T(1024)}, u32[]{:S(2)}) copy-start(f32[1536]{0:T(1024)} %copy-done.54) | copy-start | bytes 18436
  185.5 90.4 %copy-start.57 = (f32[1536]{0:T(1024)S(1)}, f32[1536]{0:T(1024)}, u32[]{:S(2)}) copy-start(f32[1536]{0:T(1024)} %copy-done.56) | copy-start | bytes 18436
  185.5 90.4 %copy-start.59 = (f32[1536]{0:T(1024)S(1)}, f32[1536]{0:T(1024)}, u32[]{:S(2)}) copy-start(f32[1536]{0:T(1024)} %copy-done.58) | copy-start | bytes 18436
  185.5 90.4 %copy-start.61 = (f32[1536]{0:T(1024)S(1)}, f32[1536]{0:T(1024)}, u32[]{:S(2)}) copy-start(f32[1536]{0:T(1024)} %copy-done.60) | copy-start | bytes 18436
  185.5 90.4 %copy-start.68 = (f32[128]{0:T(128)S(1)}, f32[128]{0:T(128)}, u32[]{:S(2)}) copy-start(f32[128]{0:T(128)} %copy-done.66) | copy-start | bytes 1540
  185.6 90.4 %copy-start.73 = (f32[128]{0:T(128)S(1)}, f32[128]{0:T(128)}, u32[]{:S(2)}) copy-start(f32[128]{0:T(128)} %copy-done.71) | copy-start | bytes 1540
  185.6 90.4 %copy-start.76 = (f32[128]{0:T(128)S(1)}, f32[128]{0:T(128)}, u32[]{:S(2)}) copy-start(f32[128]{0:T(128)} %copy-done.74) | copy-start | bytes 1540
  185.6 90.4 %copy-start.95 = (f32[128]{0:T(128)S(1)}, f32[128]{0:T(128)}, u32[]{:S(2)}) copy-start(f32[128]{0:T(128)} %copy-done.93) | copy-start | bytes 1540
  185.6 89.9 %collective-permute-start.3 = (bf16[15,1536]{1,0:T(8,128)(2,1)S(1)}, bf16[15,1536]{1,0:T(8,128)(2,1)S(1)}, u32[]{:S(2)}, u32[]{:S(2)}) collective-permute-start(bf16[15,1536]{1,0:T(8,128)(2,1)S(1)} %get-tuple-element.81), channel_id=1, source_target_pairs={{1,0},{2,1},{3,2},{4,3},{5,4},{6,5},{7,6},{8,7},{9,8},{10,9},{11,1... | collective-permute-start | bytes 138248 | tf_op jit(solution)/shard_map/ppermute | solution.py:17
  (47 other events, 233.9 us)
Sparse Core Ops, SparseCore 0:
  192.0 251.8 all-reduce.2
where the time goes:
time: 461 us; the launch traced here: 454 us
  waiting for transfers between devices  199 us (43%)
  blocking collectives  83.7 us (18%)
  starting transfers between devices  46.4 us (10%)
  other arithmetic  45.7 us (10%)
  local copies, waits for them, and re-layouts  32.9 us (7%)
  matrix products  30.7 us (7%)
  between operations  16.2 us (4%)
    psum x1, waiting for transfers between devices, on_device(): lax.psum((d_kernel, d_gain, d_router), ('tm', 'expert'))  162 us
    psum x1, blocking collectives, on_device(): lax.psum((d_kernel, d_gain, d_router), ('tm', 'expert'))  83.7 us
    all_to_all x4, waiting for transfers between devices, trade_rows(): lax.all_to_all(buffer, 'expert', split_axis=0, concat_axis=0, tiled=True)  36.3 us
    all_to_all x4, starting transfers between devices, trade_rows(): lax.all_to_all(buffer, 'expert', split_axis=0, concat_axis=0, tiled=True)  22.1 us
    dot_general x2, matrix products, expert_rows(): jnp.einsum('sjcd,jdf->sjcf', rows_in, w_up, preferred_element_type=jnp.fl...  16.4 us
    psum x1, starting transfers between devices, on_device(): lax.psum((d_kernel, d_gain, d_router), ('tm', 'expert'))  11 us
    ppermute x2, starting transfers between devices, with_halo(): lax.ppermute(lax.slice_in_dim(block, block.shape[dim] - width, None, axis...  9.34 us
  transfers between devices with their start and end apart: 9, of which 5 were waited for; matrix products, arithmetic and copies ran while one was open for 13% of the time, Pallas kernels for 0%

commit v1 on v0

v1 whole, which is shorter than its diff:
```python
import jax
import jax.numpy as jnp
from jax import lax
from jax.experimental import pallas as pl
from jax.experimental.pallas import tpu as pltpu
from jax.sharding import PartitionSpec as P

EPS = 1e-06
MESH = pl.DeviceIdType.MESH
F32, BF16 = jnp.float32, jnp.bfloat16
EXACT = lax.Precision.HIGHEST

ROWS = 128
D = 1536
TAPS = 31
EDGE = 16
WIDE = ROWS + 2 * EDGE
SPREAD = WIDE + EDGE
MID = ROWS + EDGE
EXPERTS = 16
CAP = 32
SLOTS = EXPERTS * CAP
LANES = 128
BLOCKS = D // LANES
TILE = 256
TILES = D // TILE
GRADS = 48

NT = (((1,), (1,)), ((), ()))


def sigmoid(v):
    return 0.5 * jnp.tanh(0.5 * v) + 0.5


def spread(wide, bound):
    zeros = jnp.zeros((EDGE, LANES), F32)
    before = jnp.concatenate([wide, zeros], axis=0)
    after = jnp.concatenate([zeros, wide], axis=0)
    row = lax.broadcasted_iota(jnp.int32, (SPREAD, LANES), 0)
    return jnp.where(row < bound, before, jnp.where(row >= bound + EDGE, after, 0.0))


def gather_back(mid, bound):
    row = lax.broadcasted_iota(jnp.int32, (ROWS, LANES), 0) + EDGE
    return jnp.where(row < bound, mid[:ROWS], mid[EDGE:])


def correlate(ref, block, weight_row):
    total = None
    for shift in range(8):
        rows = ref[block, shift : shift + MID + 24, :]
        for whole in range(4):
            tap = 8 * whole + shift - 1
            if 0 <= tap < TAPS:
                term = weight_row(tap) * rows[8 * whole : 8 * whole + MID]
                total = term if total is None else total + term
    return total


def body(
    len_ref, ids_ref, wconv_ref, gain_ref, wr_ref, frames_hbm, cot_hbm, wup_hbm, wdn_hbm,
    out_hbm, dfr_hbm, grad_ref,
    fr, cot, wup, wdn, gw, gd, pre, mixed, dmix, outv, dfrv, normed, cotb,
    onehot, pick, send_c, recv_c, send_x, recv_x, ret_y, got_y, ret_d, got_d,
    dhid, hid, dup, py, pd, parts,
    halo_s, halo_r, ar_src, ar_in, mid_src, mid_in, fin_src, fin,
    lsem, ssem, rsem, hs, hr, a1s, a1r, a2s, a2r, a3s, a3r,
):
    tm, ex = lax.axis_index("tm"), lax.axis_index("expert")
    xl, z = tm // 8, tm % 8
    y, xh, core = ex // 4, (ex // 2) % 2, ex % 2
    lin = tm * EXPERTS + ex

    def peer(r):
        dy, fx, dc = r // 4, (r // 2) % 2, r % 2
        return {
            "tm": ((xl + fx) % 2) * 8 + z,
            "expert": ((y + dy) % 4) * 4 + ((xh + fx) % 2) * 2 + (core + dc) % 2,
        }

    def back(r):
        return ((4 - r // 4) % 4) * 4 + r % 4

    def of_expert(e):
        return ((e // 4 + 4 - y) % 4) * 4 + ((e // 2 + xh) % 2) * 2 + (e + core) % 2

    def column(k):
        return {"tm": (tm + k) % 16, "expert": ex}

    def beside(step):
        other = (lin + 256 + step) % 256
        return {"tm": other // EXPERTS, "expert": other % EXPERTS}

    loads = [
        pltpu.make_async_copy(frames_hbm, fr, lsem.at[0]),
        pltpu.make_async_copy(cot_hbm, cot, lsem.at[1]),
        pltpu.make_async_copy(wdn_hbm.at[0], wdn, lsem.at[2]),
        pltpu.make_async_copy(wup_hbm.at[0], wup, lsem.at[3]),
    ]
    for load in loads:
        load.start()

    barrier = pltpu.get_barrier_semaphore()

    def greet(k, carry):
        pl.semaphore_signal(barrier, inc=1, device_id=peer(k), device_id_type=MESH)
        pl.semaphore_signal(barrier, inc=1, device_id=column(k), device_id_type=MESH)
        return carry

    lax.fori_loop(1, 16, greet, 0)
    pl.semaphore_signal(barrier, inc=1, device_id=beside(1), device_id_type=MESH)
    pl.semaphore_signal(barrier, inc=1, device_id=beside(-1), device_id_type=MESH)

    def upright(row):
        return jnp.broadcast_to(row.astype(F32), (LANES, ROWS)).T.astype(jnp.int32)

    ids0, ids1 = upright(ids_ref[0:1, :]), upright(ids_ref[1:2, :])

    def relative(e):
        return (
            ((((e >> 2) - y) & 3) << 2) | ((((e >> 1) & 1) ^ xh) << 1) | ((e & 1) ^ core)
        )

    rel0, rel1 = relative(ids0), relative(ids1)
    lane = lax.broadcasted_iota(jnp.int32, (ROWS, LANES), 1)
    sub = lax.broadcasted_iota(jnp.int32, (ROWS, LANES), 0)
    names0 = jnp.where(rel0 == lane, 1.0, 0.0).astype(F32)
    names1 = jnp.where(rel1 == lane, 1.0, 0.0).astype(F32)
    names = names0 + names1
    earlier = jnp.where(lane < sub, 1.0, 0.0).astype(F32)
    later = jnp.where(sub < lane, 1.0, 0.0).astype(F32)
    rank = jnp.dot(earlier.astype(BF16), names.astype(BF16), preferred_element_type=F32)
    rank0 = jnp.sum(names0 * rank, axis=1, keepdims=True).astype(jnp.int32)
    rank1 = jnp.sum(names1 * rank, axis=1, keepdims=True).astype(jnp.int32)
    slot0, slot1 = rel0 * CAP + rank0, rel1 * CAP + rank1
    for b in range(4):
        here = slice(b * LANES, (b + 1) * LANES)
        pick[0:ROWS, here] = jnp.where(lane + b * LANES == slot0, 1.0, 0.0).astype(BF16)
        pick[ROWS : 2 * ROWS, here] = jnp.where(lane + b * LANES == slot1, 1.0, 0.0).astype(BF16)
    by_expert = names.T
    order = jnp.dot(by_expert.astype(BF16), later.astype(BF16), preferred_element_type=F32)
    order = jnp.where(by_expert > 0.5, order, -1.0)
    place = lax.broadcasted_iota(jnp.int32, (CAP, LANES), 0).astype(F32)
    for r in range(EXPERTS):
        onehot[r * CAP : (r + 1) * CAP, :] = jnp.where(
            order[r : r + 1, :] == place, 1.0, 0.0
        ).astype(BF16)

    loads[0].wait()
    halo_s[0] = fr[0:EDGE, :].astype(BF16)
    halo_s[1] = fr[ROWS - EDGE : ROWS, :].astype(BF16)

    def halo(stage, side):
        n = 2 * stage + side
        return pltpu.make_async_remote_copy(
            src_ref=halo_s.at[n],
            dst_ref=halo_r.at[2 * stage + 1 - side],
            send_sem=hs.at[n],
            recv_sem=hr.at[2 * stage + 1 - side],
            device_id=beside(2 * side - 1),
            device_id_type=MESH,
        )

    pl.semaphore_wait(barrier, 32)
    halo(0, 0).start()
    halo(0, 1).start()

    def rows_of(ref, r):
        return ref.at[pl.ds(pl.multiple_of(r * CAP, CAP), CAP), :]

    def trade(kind, src, dst, r):
        return pltpu.make_async_remote_copy(
            src_ref=rows_of(src, r),
            dst_ref=rows_of(dst, back(r)),
            send_sem=ssem.at[kind, r],
            recv_sem=rsem.at[kind, back(r)],
            device_id=peer(r),
            device_id_type=MESH,
        )

    def start_batch(kind, src, dst, b):
        def one(i, carry):
            r = 4 * b + i

            @pl.when(r != 0)
            def _():
                trade(kind, src, dst, r).start()

            return carry

        lax.fori_loop(0, 4, one, 0)

    def arrive_batch(kind, src, dst, b):
        def one(i, carry):
            r = 4 * b + i

            @pl.when(r != 0)
            def _():
                trade(kind, src, dst, back(r)).wait_recv()

            return carry

        lax.fori_loop(0, 4, one, 0)

    def cols(n, width=TILE):
        return pl.ds(pl.multiple_of(n * width, width), width)

    def batch(b):
        return pl.ds(pl.multiple_of(b * ROWS, ROWS), ROWS)

    def dispatch(kind, source, src, dst):
        def one(b, carry):
            def part(n, inner):
                src[batch(b), cols(n)] = jnp.dot(
                    onehot[batch(b), :], source[:, cols(n)], preferred_element_type=F32
                ).astype(BF16)
                return inner

            lax.fori_loop(0, TILES, part, 0)
            start_batch(kind, src, dst, b)
            return carry

        lax.fori_loop(0, 4, one, 0)
        dst[0:CAP, :] = src[0:CAP, :]

    loads[1].wait()

    def narrow(n, carry):
        cotb[:, cols(n)] = cot[:, cols(n)].astype(BF16)
        return carry

    lax.fori_loop(0, TILES, narrow, 0)
    dispatch(0, cotb, send_c, recv_c)

    bound = len_ref[0] - lin * ROWS + EDGE
    bound = jnp.where((bound >= 1) & (bound < WIDE), bound, 4 * SPREAD)
    halo(0, 1).wait_recv()
    halo(0, 0).wait_recv()

    def widen(n, middle, stage, m):
        low = jnp.where(lin == 0, 0.0, halo_r[2 * stage, :, cols(m, LANES)].astype(F32))
        high = jnp.where(lin == 255, 0.0, halo_r[2 * stage + 1, :, cols(m, LANES)].astype(F32))
        return jnp.concatenate([low, middle, high], axis=0)

    def conv(m, squares):
        here = cols(m, LANES)
        gw[m] = spread(widen(0, fr[:, here], 0, m), bound)
        total = correlate(gw, m, lambda tap: wconv_ref[tap : tap + 1, here])
        act = gather_back(total, bound)
        row = fr[:, here] + act * sigmoid(act)
        pre[:, here] = act
        mixed[:, here] = row
        return squares + row * row

    squares = lax.fori_loop(0, BLOCKS, conv, jnp.zeros((ROWS, LANES), F32))
    inv = lax.rsqrt(jnp.sum(squares, axis=1, keepdims=True) * (1.0 / D) + EPS)

    def norm(m, carry):
        here = cols(m, LANES)
        normed[:, here] = (mixed[:, here] * inv * gain_ref[:, here]).astype(BF16)
        return carry

    lax.fori_loop(0, BLOCKS, norm, 0)
    dispatch(1, normed, send_x, recv_x)

    logits = lax.dot_general(
        normed[...].astype(F32), wr_ref[...], NT, precision=EXACT, preferred_element_type=F32
    )
    lane16 = lane[:, 0:EXPERTS]
    ids16 = ids0[:, 0:EXPERTS], ids1[:, 0:EXPERTS]
    top0 = jnp.sum(jnp.where(ids16[0] == lane16, logits, 0.0), axis=1, keepdims=True)
    top1 = jnp.sum(jnp.where(ids16[1] == lane16, logits, 0.0), axis=1, keepdims=True)
    most = jnp.maximum(top0, top1)
    exp0, exp1 = jnp.exp(top0 - most), jnp.exp(top1 - most)
    gate0, gate1 = exp0 / (exp0 + exp1), exp1 / (exp0 + exp1)

    loads[2].wait()

    def hidden_grad(b, carry):
        arrive_batch(0, send_c, recv_c, b)

        def part(n, inner):
            dhid[batch(b), cols(n)] = lax.dot_general(
                recv_c[batch(b), :], wdn[cols(n), :], NT, preferred_element_type=F32
            ).astype(BF16)
            return inner

        lax.fori_loop(0, TILES, part, 0)
        return carry

    lax.fori_loop(0, 4, hidden_grad, 0)
    loads[3].wait()

    def expert(b, carry):
        arrive_batch(1, send_x, recv_x, b)

        def up(n, inner):
            u = jnp.dot(recv_x[batch(b), :], wup[:, cols(n)], preferred_element_type=F32)
            s = sigmoid(u)
            hid[:, cols(n)] = (u * s).astype(BF16)
            slope = s * (1.0 + u * (1.0 - s))
            dup[:, cols(n)] = (dhid[batch(b), cols(n)].astype(F32) * slope).astype(BF16)
            return inner

        def down(n, inner):
            ret_y[batch(b), cols(n)] = jnp.dot(
                hid[...], wdn[:, cols(n)], preferred_element_type=F32
            ).astype(BF16)
            return inner

        def rows_grad(n, inner):
            ret_d[batch(b), cols(n)] = lax.dot_general(
                dup[...], wup[cols(n), :], NT, preferred_element_type=F32
            ).astype(BF16)
            return inner

        lax.fori_loop(0, TILES, up, 0)
        lax.fori_loop(0, TILES, down, 0)
        start_batch(2, ret_y, got_y, b)
        lax.fori_loop(0, TILES, rows_grad, 0)
        start_batch(3, ret_d, got_d, b)
        return carry

    lax.fori_loop(0, 4, expert, 0)
    got_y[0:CAP, :] = ret_y[0:CAP, :]
    got_d[0:CAP, :] = ret_d[0:CAP, :]

    def collect(kind, src, got, total):
        for b in range(4):
            arrive_batch(kind, src, got, b)

            def part(n, carry):
                term = jnp.dot(
                    pick[:, b * ROWS : (b + 1) * ROWS],
                    got[batch(b), cols(n)],
                    preferred_element_type=F32,
                )
                total[:, cols(n)] = term if b == 0 else total[:, cols(n)] + term
                return carry

            lax.fori_loop(0, TILES, part, 0)

    collect(2, ret_y, got_y, py)

    def finish(m, sums):
        here = cols(m, LANES)
        first, second = py[0:ROWS, here], py[ROWS : 2 * ROWS, here]
        outv[:, here] = mixed[:, here] + (gate0 * first + gate1 * second)
        c = cot[:, here]
        return sums + c * (first - second)

    sums = lax.fori_loop(0, BLOCKS, finish, jnp.zeros((ROWS, LANES), F32))
    store_out = pltpu.make_async_copy(outv, out_hbm, lsem.at[4])
    store_out.start()
    dtop = gate0 * gate1 * jnp.sum(sums, axis=1, keepdims=True)
    dlogits = jnp.where(ids0 == lane, dtop, 0.0) - jnp.where(ids1 == lane, dtop, 0.0)
    dlogits_t = dlogits.T[0:EXPERTS, :]
    dlogits = dlogits[:, 0:EXPERTS]

    def router(m, carry):
        here = cols(m, LANES)
        ar_src[m, 32:48, :] = jnp.dot(
            dlogits_t, normed[:, here].astype(F32), precision=EXACT, preferred_element_type=F32
        ).astype(BF16)
        dmix[:, here] = jnp.dot(
            dlogits, wr_ref[:, here], precision=EXACT, preferred_element_type=F32
        )
        return carry

    lax.fori_loop(0, BLOCKS, router, 0)

    collect(3, ret_d, got_d, pd)

    def norm_back(m, sums):
        here = cols(m, LANES)
        dn = gate0 * pd[0:ROWS, here] + gate1 * pd[ROWS : 2 * ROWS, here] + dmix[:, here]
        row = mixed[:, here]
        parts[m, 0:8, :] = jnp.sum((dn * row * inv).reshape(ROWS // 8, 8, LANES), axis=0)
        dn = dn * gain_ref[:, here]
        pd[0:ROWS, here] = dn
        return sums + dn * row

    sums = lax.fori_loop(0, BLOCKS, norm_back, jnp.zeros((ROWS, LANES), F32))
    pull = inv * inv * inv * (jnp.sum(sums, axis=1, keepdims=True) * (1.0 / D))

    def act_back(m, carry):
        here = cols(m, LANES)
        dm = cot[:, here] + (inv * pd[0:ROWS, here] - mixed[:, here] * pull)
        act = pre[:, here]
        s = sigmoid(act)
        dp = dm * (s * (1.0 + act * (1.0 - s)))
        dmix[:, here] = dm
        pd[ROWS : 2 * ROWS, here] = dp
        halo_s[2, :, here] = dp[0:EDGE].astype(BF16)
        halo_s[3, :, here] = dp[ROWS - EDGE : ROWS].astype(BF16)
        return carry

    lax.fori_loop(0, BLOCKS, act_back, 0)
    halo(1, 0).start()
    halo(1, 1).start()

    rows32 = lax.broadcasted_iota(jnp.int32, (32, 256), 0)
    lanes32 = lax.broadcasted_iota(jnp.int32, (32, 256), 1)
    fold = jnp.where((lanes32 >> 3) == rows32, 1.0, 0.0).astype(F32)

    def to_owner(m):
        r = of_expert(m)
        return pltpu.make_async_remote_copy(
            src_ref=ar_src.at[m],
            dst_ref=ar_in.at[back(r)],
            send_sem=a1s.at[m],
            recv_sem=a1r.at[back(r)],
            device_id=peer(r),
            device_id_type=MESH,
        )

    def kernel_grad(i, carry):
        m = (i + ex) % BLOCKS
        here = cols(m, LANES)
        edge = jnp.zeros((EDGE, LANES), F32)
        mid = spread(jnp.concatenate([edge, pd[ROWS : 2 * ROWS, here], edge], axis=0), bound)
        mid = mid[EDGE : EDGE + MID]
        terms = [None] * TAPS
        for shift in range(8):
            rows = gw[m, shift : shift + MID + 24, :]
            for whole in range(4):
                tap = 8 * whole + shift - 1
                if 0 <= tap < TAPS:
                    product = mid * rows[8 * whole : 8 * whole + MID]
                    terms[tap] = jnp.sum(product.reshape(MID // 8, 8, LANES), axis=0)
        terms.append(parts[m, 0:8, :])
        ar_src[m, 0:32, :] = jnp.dot(
            fold, jnp.concatenate(terms, axis=0), precision=EXACT, preferred_element_type=F32
        ).astype(BF16)

        @pl.when(m != ex)
        def _():
            to_owner(m).start()

        return carry

    lax.fori_loop(0, BLOCKS, kernel_grad, 0)

    halo(1, 1).wait_recv()
    halo(1, 0).wait_recv()

    def frames_back(m, carry):
        here = cols(m, LANES)
        gd[0] = spread(widen(0, pd[ROWS : 2 * ROWS, here], 1, m), bound)
        total = correlate(gd, 0, lambda tap: wconv_ref[TAPS - 1 - tap : TAPS - tap, here])
        dfrv[:, here] = dmix[:, here] + gather_back(total, bound)
        return carry

    lax.fori_loop(0, BLOCKS // 2, frames_back, 0)

    def over_columns(k):
        return pltpu.make_async_remote_copy(
            src_ref=mid_src,
            dst_ref=mid_in.at[16 - k],
            send_sem=a2s.at[k],
            recv_sem=a2r.at[16 - k],
            device_id=column(k),
            device_id_type=MESH,
        )

    def to_all(r):
        return pltpu.make_async_remote_copy(
            src_ref=fin_src,
            dst_ref=fin.at[ex],
            send_sem=a3s.at[r],
            recv_sem=a3r.at[ex],
            device_id=peer(r),
            device_id_type=MESH,
        )

    @pl.when(ex < BLOCKS)
    def _():
        def add(q, total):
            pltpu.make_async_remote_copy(
                src_ref=ar_src.at[0],
                dst_ref=ar_in.at[q],
                send_sem=a1s.at[0],
                recv_sem=a1r.at[q],
                device_id=peer(q),
                device_id_type=MESH,
            ).wait_recv()
            return total + ar_in[q].astype(F32)

        total = lax.fori_loop(1, 16, add, ar_src[ex].astype(F32))
        mid_src[...] = total.astype(BF16)

        def send(k, carry):
            over_columns(k).start()
            return carry

        lax.fori_loop(1, 16, send, 0)

    lax.fori_loop(BLOCKS // 2, BLOCKS, frames_back, 0)
    store_dfr = pltpu.make_async_copy(dfrv, dfr_hbm, lsem.at[5])
    store_dfr.start()

    @pl.when(ex < BLOCKS)
    def _():
        def add(k, total):
            over_columns(16 - k).wait_recv()
            return total + mid_in[k].astype(F32)

        total = lax.fori_loop(1, 16, add, mid_src[...].astype(F32))
        fin_src[...] = total.astype(BF16)

        def send(r, carry):
            to_all(r).start()
            return carry

        lax.fori_loop(1, 16, send, 0)
        fin[ex] = fin_src[...]

    def spread_out(m, carry):
        @pl.when(m != ex)
        def _():
            pltpu.make_async_remote_copy(
                src_ref=fin_src,
                dst_ref=fin.at[m],
                send_sem=a3s.at[0],
                recv_sem=a3r.at[m],
                device_id=peer(of_expert(m)),
                device_id_type=MESH,
            ).wait_recv()

        grad_ref[:, cols(m, LANES)] = fin[m].astype(F32)
        return carry

    lax.fori_loop(0, BLOCKS, spread_out, 0)

    def sent(r, carry):
        trade(0, send_c, recv_c, r).wait_send()
        trade(1, send_x, recv_x, r).wait_send()
        trade(2, ret_y, got_y, r).wait_send()
        trade(3, ret_d, got_d, r).wait_send()
        return carry

    lax.fori_loop(1, 16, sent, 0)

    def sent_owner(m, carry):
        @pl.when(m != ex)
        def _():
            to_owner(m).wait_send()

        return carry

    lax.fori_loop(0, BLOCKS, sent_owner, 0)

    @pl.when(ex < BLOCKS)
    def _():
        def done(k, carry):
            over_columns(k).wait_send()
            to_all(k).wait_send()
            return carry

        lax.fori_loop(1, 16, done, 0)

    for stage in range(2):
        for side in range(2):
            halo(stage, side).wait_send()
    store_out.wait()
    store_dfr.wait()


def on_device(frames, lengths, expert_ids, w_conv, g_norm, w_router, w_up, w_down, cotangent):
    vmem = pl.BlockSpec(memory_space=pltpu.VMEM)
    smem = pl.BlockSpec(memory_space=pltpu.SMEM)
    anywhere = pl.BlockSpec(memory_space=pl.ANY)
    wide_f = pltpu.VMEM((ROWS, D), F32)
    slots = pltpu.VMEM((SLOTS, D), BF16)
    weight = pltpu.VMEM((D, D), BF16)
    dma = pltpu.SemaphoreType.DMA
    block_out, frames_grad, grads = pl.pallas_call(
        body,
        out_shape=(
            jax.ShapeDtypeStruct((ROWS, D), F32),
            jax.ShapeDtypeStruct((ROWS, D), F32),
            jax.ShapeDtypeStruct((GRADS, D), F32),
        ),
        in_specs=[smem, vmem, vmem, vmem, vmem, anywhere, anywhere, anywhere, anywhere],
        out_specs=(anywhere, anywhere, vmem),
        scratch_shapes=[
            wide_f, wide_f, weight, weight,
            pltpu.VMEM((BLOCKS, SPREAD, LANES), F32),
            pltpu.VMEM((1, SPREAD, LANES), F32),
            wide_f, wide_f, wide_f, wide_f, wide_f,
            pltpu.VMEM((ROWS, D), BF16), pltpu.VMEM((ROWS, D), BF16),
            pltpu.VMEM((SLOTS, ROWS), BF16), pltpu.VMEM((2 * ROWS, SLOTS), BF16),
            slots, slots, slots, slots, slots, slots, slots, slots,
            slots, pltpu.VMEM((ROWS, D), BF16), pltpu.VMEM((ROWS, D), BF16),
            pltpu.VMEM((2 * ROWS, D), F32), pltpu.VMEM((2 * ROWS, D), F32),
            pltpu.VMEM((BLOCKS, 8, LANES), F32),
            pltpu.VMEM((4, EDGE, D), BF16), pltpu.VMEM((4, EDGE, D), BF16),
            pltpu.VMEM((BLOCKS, GRADS, LANES), BF16), pltpu.VMEM((16, GRADS, LANES), BF16),
            pltpu.VMEM((GRADS, LANES), BF16), pltpu.VMEM((16, GRADS, LANES), BF16),
            pltpu.VMEM((GRADS, LANES), BF16), pltpu.VMEM((BLOCKS, GRADS, LANES), BF16),
            dma((6,)), dma((4, 16)), dma((4, 16)), dma((4,)), dma((4,)),
            dma((BLOCKS,)), dma((16,)), dma((16,)), dma((16,)), dma((16,)), dma((BLOCKS,)),
        ],
        compiler_params=pltpu.CompilerParams(
            collective_id=0, has_side_effects=True, vmem_limit_bytes=56 * 2**20
        ),
    )(
        lengths, expert_ids.T, w_conv, g_norm.reshape(1, D), w_router.T,
        frames, cotangent, w_up, w_down,
    )
    return block_out, frames_grad, grads[:TAPS], grads[TAPS], grads[32:].T


def solution(mesh):
    placed = (
        P(("tm", "expert"), None),
        P(),
        P(("tm", "expert"), None),
        P(),
        P(),
        P(),
        P("expert", None, None),
        P("expert", None, None),
        P(("tm", "expert"), None),
    )
    return jax.shard_map(
        on_device,
        mesh=mesh,
        in_specs=placed,
        out_specs=(P(("tm", "expert"), None), P(("tm", "expert"), None), P(), P(), P()),
        check_vma=False,
    )
```

time: 461 us -> 142 us (0.31); the launches traced: 454 us -> 142 us
  waiting for transfers between devices: 199 us -> 0 us
  Pallas kernels: 0 us -> 132 us
  blocking collectives: 83.7 us -> 0 us
  starting transfers between devices: 46.4 us -> 0 us
  other arithmetic: 45.7 us -> 0 us
  matrix products: 30.7 us -> 0 us
  local copies, waits for them, and re-layouts: 32.9 us -> 10 us
  between operations: 16.2 us -> 0.64 us
    psum x1 -> x0, waiting for transfers between devices: 162 us -> none  [on_device(): lax.psum((d_kernel, d_gain, d_router), ('tm', 'expert'))]
    pallas_call x0 -> x1, Pallas kernels: none -> 132 us  [on_device(): pl.pallas_call(body, out_shape=(jax.ShapeDtypeStruct((ROWS, D), F32), jax...]
    psum x1 -> x0, blocking collectives: 83.7 us -> none  [on_device(): lax.psum((d_kernel, d_gain, d_router), ('tm', 'expert'))]
    all_to_all x4 -> x0, waiting for transfers between devices: 36.3 us -> none  [trade_rows(): lax.all_to_all(buffer, 'expert', split_axis=0, concat_axis=0, tiled=True)]
    dot_general x8 -> x0, matrix products: 30.7 us -> none  [the longest x2 16.4 us: expert_rows(): jnp.einsum('sjcd,jdf->sjcf', rows_in, w_up, preferred_element_type=jnp.fl...]
    reduce_sum x10 -> x0, other arithmetic: 24.8 us -> none  [the longest x1 7.99 us: norm_rows(): inv_scale = lax.rsqrt(jnp.mean(mixed * mixed, axis=-1, keepdims=True) + EPS)]
    all_to_all x4 -> x0, starting transfers between devices: 22.1 us -> none  [trade_rows(): lax.all_to_all(buffer, 'expert', split_axis=0, concat_axis=0, tiled=True)]
    ppermute x4 -> x0, starting transfers between devices: 13.3 us -> none  [the longest x2 9.34 us: with_halo(): lax.ppermute(lax.slice_in_dim(block, block.shape[dim] - width, None, axis...]
  transfers between devices with their start and end apart: 9 -> 0, of which waited for: 5 -> 0; matrix products, arithmetic and copies ran while one was open for 13% -> 0% of each run, Pallas kernels for 0% -> 0%
where the time goes in v1:
time: 142 us
  Pallas kernels  132 us (93%)
  local copies, waits for them, and re-layouts  10 us (7%)
    pallas_call x1, Pallas kernels, on_device(): pl.pallas_call(body, out_shape=(jax.ShapeDtypeStruct((ROWS, D), F32), jax...  132 us
    unnamed x2, local copies, waits for them, and re-layouts  4.14 us
    slice x2, local copies, waits for them, and re-layouts, on_device(): return (block_out, frames_grad, grads[:TAPS], grads[TAPS], grads[32:].T)  3.03 us

profile of v1, /device:TPU:1, one launch (start us, length us, event | category | flops | bytes accessed | tf_op | source)
XLA Modules:
  0.0 142.1 jit_solution(9093345019612136518)
XLA Ops:
  0.6 1.3 reshape.13.gain_ref
  1.9 131.5 %shard_map.128 = (f32[128,1536]{1,0:T(8,128)}, f32[128,1536]{1,0:T(8,128)}, f32[48,1536]{1,0:T(8,128)}) custom-call(s32[2]{0:T(128)} %len_ref.1, s32[2,128]{1,0:T(2,128)} %bitcast.5, f32[31,1536]{1,0:T(8,128)} %wconv_ref.1, f32[1,1536]{1,0:T(1,128)} %reshape.13.gain_ref, f32[16,1536]{1,0:T(8,128)} %bitcast.4, f32[128,1536]{1,0:T(8,128)} %frames_hbm.1, ...), custom_call_target="tpu_custom_call" | custom-call | tf_op jit(solution)/shard_map/pallas_call | solution.py:578
  133.4 1.6 %slice.9 = f32[31,1536]{1,0:T(8,128)} slice(f32[48,1536]{1,0:T(8,128)} %get-tuple-element.10), slice={[0:31], [0:1536]} | slice | bytes 380928 | tf_op jit(solution)/shard_map/slice | solution.py:612
  135.1 1.4 slice_reduce_fusion
  136.5 1.5 %slice_bitcast_fusion = f32[1536,16]{0,1:T(8,128)} fusion(f32[48,1536]{1,0:T(8,128)} %get-tuple-element.10), kind=kLoop, calls=%fused_computation | loop fusion | bytes 196608 | tf_op jit(solution)/shard_map/transpose | solution.py:612
  138.0 2.1 %copy.16 = f32[128,1536]{1,0:T(8,128)} copy(f32[128,1536]{1,0:T(8,128)} %get-tuple-element.16) | data formatting | bytes 1572864
  140.1 2.1 %copy.17 = f32[128,1536]{1,0:T(8,128)} copy(f32[128,1536]{1,0:T(8,128)} %get-tuple-element.17) | data formatting | bytes 1572864
